TPU v7x, 32 devices: a whole 2x2x4 slice. The times are simulated.
32 devices in a mesh: ctx: 8 (over y, x, core), ch: 4 (over z).
Axes of the slice: x: 2, y: 2, z: 4, core: 2. Of those that a mesh axis runs over, the one named last changes fastest.
Arguments:
- query_in: bfloat16 [1536, 8192], P('ctx', 'ch'), may hold values from -6 to 6
- key_in: bfloat16 [1536, 8192], P('ctx', 'ch'), may hold values from -6 to 6
- value_in: bfloat16 [1536, 8192], P('ctx', 'ch'), may hold values from -6 to 6
- filters: bfloat16 [512, 1536], P('ch'), may hold values from -0.8 to 0.8
- skip_gain: float32 [8192], P('ch'), may hold values from -3 to 3
- out_weight: bfloat16 [8192, 8192], P(None, 'ch'), may hold values from -0.0625 to 0.0625
Outputs:
- output: bfloat16 [1536, 8192], P('ctx', 'ch')
All inputs are finite; a program needn't handle non-finite values.
Results may differ from a plain program's by a relative error of at most 0.0057.
Values may be sent and summed in bfloat16 or wider, within the bound.
A program may use at most 128 MiB of HBM per device.

v0:
```python
import jax
import jax.numpy as jnp
from jax import lax
from jax.sharding import PartitionSpec as P


def toeplitz(padded, offset, out_rows, src_rows):
    groups = padded.shape[0]
    seq_len = padded.shape[1] // 2
    width = out_rows + src_rows - 1
    segment = lax.dynamic_slice_in_dim(padded, offset - src_rows + 1 + seq_len, width, 1)
    flipped = jnp.concatenate([segment[:, ::-1], jnp.zeros((groups, 1), segment.dtype)], axis=1)
    period = width + 1
    repeated = jnp.broadcast_to(flipped[:, None, :], (groups, out_rows, period)).reshape(
        groups, out_rows * period
    )
    sheared = repeated[:, out_rows - 1 : out_rows - 1 + out_rows * width].reshape(
        groups, out_rows, width
    )
    return sheared[:, :, :src_rows]


def apply_gate(query_part, conv, gain, mixed_part):
    total = conv + gain[None, :] * mixed_part.astype(jnp.float32)
    return (query_part.astype(jnp.float32) * total).astype(jnp.bfloat16)


def project(gated, out_weight):
    total = jnp.dot(
        lax.all_gather(gated, "ch", axis=1, tiled=True),
        out_weight,
        preferred_element_type=jnp.float32,
    )
    return total.astype(jnp.bfloat16)


def shards(query_in, key_in, value_in, filters, skip_gain, out_weight):
    block_rows = query_in.shape[0]
    channels = query_in.shape[1]
    cycle_size = lax.axis_size("ctx")
    cycle_pos = lax.axis_index("ctx")
    seq_len = block_rows * cycle_size
    group_width = channels // filters.shape[0]
    mixed = (key_in.astype(jnp.float32) * value_in.astype(jnp.float32)).astype(jnp.bfloat16)
    padded = jnp.concatenate([jnp.zeros_like(filters), filters], axis=1)
    narrow = channels // cycle_size
    sub_groups = narrow // group_width
    query_ch, mixed_ch = (
        lax.all_to_all(query_in, "ctx", split_axis=1, concat_axis=0, tiled=True),
        lax.all_to_all(mixed, "ctx", split_axis=1, concat_axis=0, tiled=True),
    )
    padded_sub = lax.dynamic_slice_in_dim(padded, cycle_pos * sub_groups, sub_groups, 0)
    gain_sub = lax.dynamic_slice_in_dim(skip_gain, cycle_pos * narrow, narrow, 0)
    tile_rows = min(512, seq_len)
    block_count = seq_len // tile_rows
    stacked = mixed_ch.reshape(block_count, tile_rows, sub_groups, group_width)
    block_ids = jnp.arange(block_count, dtype=jnp.int32)

    def offset_step(summed, offset):
        tiles = toeplitz(padded_sub, offset * tile_rows, tile_rows, tile_rows)
        result = jnp.einsum("grs,nsgc->nrgc", tiles, stacked, preferred_element_type=jnp.float32)
        shifted = jnp.roll(result, offset, axis=0)
        keep = (block_ids >= offset)[:, None, None, None]
        return (summed + jnp.where(keep, shifted, 0.0), None)

    start_sum = jnp.zeros((block_count, tile_rows, sub_groups, group_width), jnp.float32)
    summed, _ = lax.scan(offset_step, start_sum, block_ids)
    conv = summed.reshape(seq_len, narrow)
    gated_ch = apply_gate(query_ch, conv, gain_sub, mixed_ch)
    gated = lax.all_to_all(gated_ch, "ctx", split_axis=0, concat_axis=1, tiled=True)
    return project(gated, out_weight)


def solution(mesh):
    placed = (P("ctx", "ch"), P("ctx", "ch"), P("ctx", "ch"), P("ch", None), P("ch"), P(None, "ch"))
    return jax.shard_map(
        shards, mesh=mesh, in_specs=placed, out_specs=P("ctx", "ch"), check_vma=False
    )
```

profile of v0, /device:TPU:0, one launch (start us, length us, event | category | flops | bytes accessed | tf_op | source)
XLA Modules:
  0.0 438.1 jit_solution(18237333984734716645)
XLA Ops:
  6.5 1.6 multiply_convert_fusion
  8.2 0.0 copy-start.2
  8.2 0.9 copy.40
  9.1 5.2 %all-to-all-start.1 = ((bf16[192,8,256]{2,0,1:T(8,128)(2,1)}), bf16[192,8,256]{2,0,1:T(8,128)(2,1)S(1)}, u32[]{:S(2)}, u32[]{:S(2)}) async-start(bf16[192,8,256]{2,0,1:T(8,128)(2,1)} %bitcast.33), calls=%async_computation.1 | async-start | bytes 1572864 | tf_op jit(solution)/shard_map/all_to_all | solution.py:50
  14.3 0.0 copy-done.2
  14.3 1.0 copy.41
  15.3 1.3 dynamic_slice.36
  16.6 0.8 pad_dynamic-slice_fusion.2
  17.4 9.5 %all-to-all-done.1 = bf16[192,8,256]{2,0,1:T(8,128)(2,1)S(1)} async-done(((bf16[192,8,256]{2,0,1:T(8,128)(2,1)}), bf16[192,8,256]{2,0,1:T(8,128)(2,1)S(1)}, u32[]{:S(2)}, u32[]{:S(2)}) %all-to-all-start.1) | async-done | bytes 786464 | tf_op jit(solution)/shard_map/all_to_all | solution.py:50
  26.9 4.2 all-to-all-start
  31.1 0.0 all-gather.2.cloned.1.call-start
  31.2 1.7 copy.25
  32.9 0.0 copy-done
  32.9 3.0 reshape.46
  35.9 1.1 copy.26
  37.0 287.8 %while.16 = (s32[]{:T(128)}, f32[3,512,16,16]{1,3,0,2:T(8,128)S(1)}, s32[3]{0:T(128)S(1)}, bf16[16,3072]{1,0:T(8,128)(2,1)S(1)}, bf16[3,512,16,16]{1,3,0,2:T(8,1...) while((s32[]{:T(128)}, ...), condition=%wide.region_1.2_spmd.clone.clone, body=%wide.region_0.1_spmd.clone.clone.sunk | while | flops 404226048 | bytes 133136560 | solution.py:67
  37.0 0.7 dynamic_slice.64
  39.1 0.1 constant_dynamic-slice_fusion.2
  39.2 0.7 reverse.2
  39.8 0.1 slice.31
  39.9 2.2 broadcast_in_dim.54
  42.1 29.2 %copy.43 = bf16[2,8,512,1024]{3,1,2,0:T(8,128)(2,1)S(1)} copy(bf16[2,8,512,1024]{3,2,1,0:T(8,128)(2,1)S(1)} %bitcast.49) | data formatting | bytes 33554432 | tf_op jit(solution)/shard_map/while
  71.4 8.4 %slice.32 = bf16[16,523776]{1,0:T(8,128)(2,1)} slice(bf16[16,524288]{1,0:T(8,128)(2,1)S(1)} %bitcast.50), slice={[0:16], [511:524287]} | slice | bytes 33521664 | tf_op jit(solution)/shard_map/while/body/eval_jaxpr/slice | solution.py:17
  79.8 45.3 %reshape.55 = bf16[16,512,1023]{2,1,0:T(8,128)(2,1)} reshape(bf16[16,523776]{1,0:T(8,128)(2,1)} %slice.32) | data formatting | bytes 33521664 | tf_op jit(solution)/shard_map/while/body/eval_jaxpr/reshape | solution.py:17
  125.1 6.2 %fusion.15 = f32[16,512,48]{1,2,0:S(1)} fusion(bf16[16,512,48]{1,2,0:T(8,128)(2,1)} %bitcast.57, bf16[16,512,1023]{2,1,0:T(8,128)(2,1)} %reshape.55), kind=kOutput, calls=%fused_computation.clone.1 | convolution fusion | flops 402653184 | bytes 10747904 | tf_op jit(solution)/shard_map/while
  131.3 0.7 broadcast_compare_fusion.2
  132.0 0.9 fusion.16
  132.9 0.7 dynamic_slice.64
  134.9 0.1 constant_dynamic-slice_fusion.2
  135.0 0.7 reverse.2
  135.7 0.1 slice.31
  135.8 2.2 broadcast_in_dim.54
  138.0 29.2 %copy.43 = bf16[2,8,512,1024]{3,1,2,0:T(8,128)(2,1)S(1)} copy(bf16[2,8,512,1024]{3,2,1,0:T(8,128)(2,1)S(1)} %bitcast.49) | data formatting | bytes 33554432 | tf_op jit(solution)/shard_map/while
  167.2 8.4 %slice.32 = bf16[16,523776]{1,0:T(8,128)(2,1)} slice(bf16[16,524288]{1,0:T(8,128)(2,1)S(1)} %bitcast.50), slice={[0:16], [511:524287]} | slice | bytes 33521664 | tf_op jit(solution)/shard_map/while/body/eval_jaxpr/slice | solution.py:17
  175.6 45.3 %reshape.55 = bf16[16,512,1023]{2,1,0:T(8,128)(2,1)} reshape(bf16[16,523776]{1,0:T(8,128)(2,1)} %slice.32) | data formatting | bytes 33521664 | tf_op jit(solution)/shard_map/while/body/eval_jaxpr/reshape | solution.py:17
  221.0 6.2 %fusion.15 = f32[16,512,48]{1,2,0:S(1)} fusion(bf16[16,512,48]{1,2,0:T(8,128)(2,1)} %bitcast.57, bf16[16,512,1023]{2,1,0:T(8,128)(2,1)} %reshape.55), kind=kOutput, calls=%fused_computation.clone.1 | convolution fusion | flops 402653184 | bytes 10747904 | tf_op jit(solution)/shard_map/while
  227.1 0.7 broadcast_compare_fusion.2
  227.8 0.9 fusion.16
  228.7 0.7 dynamic_slice.64
  230.8 0.1 constant_dynamic-slice_fusion.2
  230.9 0.7 reverse.2
  231.5 0.1 slice.31
  231.6 2.2 broadcast_in_dim.54
  233.9 29.2 %copy.43 = bf16[2,8,512,1024]{3,1,2,0:T(8,128)(2,1)S(1)} copy(bf16[2,8,512,1024]{3,2,1,0:T(8,128)(2,1)S(1)} %bitcast.49) | data formatting | bytes 33554432 | tf_op jit(solution)/shard_map/while
  263.1 8.4 %slice.32 = bf16[16,523776]{1,0:T(8,128)(2,1)} slice(bf16[16,524288]{1,0:T(8,128)(2,1)S(1)} %bitcast.50), slice={[0:16], [511:524287]} | slice | bytes 33521664 | tf_op jit(solution)/shard_map/while/body/eval_jaxpr/slice | solution.py:17
  271.5 45.3 %reshape.55 = bf16[16,512,1023]{2,1,0:T(8,128)(2,1)} reshape(bf16[16,523776]{1,0:T(8,128)(2,1)} %slice.32) | data formatting | bytes 33521664 | tf_op jit(solution)/shard_map/while/body/eval_jaxpr/reshape | solution.py:17
  316.8 6.2 %fusion.15 = f32[16,512,48]{1,2,0:S(1)} fusion(bf16[16,512,48]{1,2,0:T(8,128)(2,1)} %bitcast.57, bf16[16,512,1023]{2,1,0:T(8,128)(2,1)} %reshape.55), kind=kOutput, calls=%fused_computation.clone.1 | convolution fusion | flops 402653184 | bytes 10747904 | tf_op jit(solution)/shard_map/while
  323.0 0.7 broadcast_compare_fusion.2
  323.7 0.9 fusion.16
  324.8 2.4 copy.27
  327.2 3.2 reshape.47
  330.4 0.0 copy-start.1
  330.4 0.0 copy-start.3
  330.4 2.0 copy.28
  332.4 0.0 all-to-all-done
  332.4 0.0 copy-done.1
  332.4 0.0 copy-done.3
  332.4 2.5 fusion.5
  334.9 0.2 copy.29
  335.1 16.4 %all_to_all.45 = bf16[8,192,256]{2,1,0:T(8,128)(2,1)S(1)} all-to-all(bf16[8,192,256]{2,1,0:T(8,128)(2,1)S(1)} %copy.29), channel_id=1, replica_groups=mesh['ctx'=8,'ch'=4] {'ctx'}, dimensions={0} | all-to-all | bytes 1572864 | tf_op jit(solution)/shard_map/all_to_all | solution.py:70
  351.5 1.0 copy.35
  352.5 0.0 all-gather.2.cloned.1.call-update
  352.5 63.0 %all-gather.2.cloned.1.call-done = bf16[192,8192]{1,0:T(8,128)(2,1)} async-done(((bf16[192,2048]{1,0:T(8,128)(2,1)}), bf16[192,8192]{1,0:T(8,128)(2,1)}) %all-gather.2.cloned.1.call-update) | async-done | bytes 3145744 | tf_op jit(solution)/shard_map/all_gather | solution.py:30
  415.5 15.7 %convolution_convert_fusion = bf16[192,2048]{1,0:T(8,128)(2,1)} fusion(bf16[192,8192]{1,0:T(8,128)(2,1)} %all-gather.2.cloned.1.call-done, bf16[8192,2048]{1,0:T(8,128)(2,1)} %param.13), kind=kOutput, calls=%fused_computation.9 | convolution fusion | flops 6442844160 | bytes 37486592 | tf_op jit(solution)/shard_map/dot_general | solution.py:29
  (6 shorter events, 0.0 us)
Async XLA Ops:
  8.2 6.1 %copy-start.2 = (bf16[192,2048]{1,0:T(8,128)(2,1)S(1)}, bf16[192,2048]{1,0:T(8,128)(2,1)}, u32[]{:S(2)}) copy-start(bf16[192,2048]{1,0:T(8,128)(2,1)} %param.8) | copy-start | bytes 2359300
  9.1 17.8 %all-to-all-start.1 = ((bf16[192,8,256]{2,0,1:T(8,128)(2,1)}), bf16[192,8,256]{2,0,1:T(8,128)(2,1)S(1)}, u32[]{:S(2)}, u32[]{:S(2)}) async-start(bf16[192,8,256]{2,0,1:T(8,128)(2,1)} %bitcast.33), calls=%async_computation.1 | async-start | bytes 1572864 | tf_op jit(solution)/shard_map/all_to_all | solution.py:50
  26.9 6.0 %copy-start = (bf16[192,8,256]{2,0,1:T(8,128)(2,1)}, bf16[192,8,256]{2,0,1:T(8,128)(2,1)S(1)}, u32[]{:S(2)}) copy-start(bf16[192,8,256]{2,0,1:T(8,128)(2,1)S(1)} %all-to-all-done.1) | copy-start | bytes 2359300
  26.9 305.5 %all-to-all-start = ((bf16[192,8,256]{2,0,1:T(8,128)(2,1)}), bf16[192,8,256]{2,0,1:T(8,128)(2,1)}, u32[]{:S(2)}, u32[]{:S(2)}) async-start(bf16[192,8,256]{2,0,1:T(8,128)(2,1)} %bitcast.34), calls=%async_computation | async-start | bytes 1572864 | tf_op jit(solution)/shard_map/all_to_all | solution.py:49
  31.1 384.4 %all-gather.2.cloned.1.call-start = ((), (), s32[]{:S(2)}) async-start(), calls=%async_computation.3 | async-start | bytes 3932160 | tf_op jit(solution)/shard_map/all_gather | solution.py:30
  330.4 2.0 copy-start.1
  330.4 2.0 copy-start.3
Sparse Core Ops, SparseCore 0:
  352.6 62.8 all-gather.1
where the time goes:
time: 439 us; the launch traced here: 438 us
  local copies, waits for them, and re-layouts  279 us (64%)
  waiting for transfers between devices  72.5 us (17%)
  matrix products  34.2 us (8%)
  blocking collectives  16.4 us (4%)
  between operations  13.5 us (3%)
  starting transfers between devices  9.44 us (2%)
  other arithmetic  8.84 us (2%)
  loops' own time  4.64 us (1%)
    reshape x3, local copies, waits for them, and re-layouts, toeplitz(): repeated[:, out_rows - 1:out_rows - 1 + out_rows * width]  136 us
    while x9, local copies, waits for them, and re-layouts  89.8 us
    all_gather x1, waiting for transfers between devices, project(): lax.all_gather(gated, 'ch', axis=1, tiled=True)  63 us
    slice x3, local copies, waits for them, and re-layouts, toeplitz(): repeated[:, out_rows - 1:out_rows - 1 + out_rows * width]  25.3 us
    while x3, matrix products  18.5 us
    all_to_all x1, blocking collectives, shards(): lax.all_to_all(gated_ch, 'ctx', split_axis=0, concat_axis=1, tiled=True)  16.4 us
    dot_general x1, matrix products, project(): jnp.dot(lax.all_gather(gated, 'ch', axis=1, tiled=True), out_weight, pref...  15.7 us
    all_to_all x1, waiting for transfers between devices, shards(): lax.all_to_all(mixed, 'ctx', split_axis=1, concat_axis=0, tiled=True)  9.47 us
  transfers between devices with their start and end apart: 3, of which 2 were waited for; matrix products, arithmetic and copies ran while one was open for 68% of the time, Pallas kernels for 0%

commit v1 on v0

v1 whole, which is shorter than its diff:
```python
import functools

import jax
import jax.numpy as jnp
from jax import lax
from jax.experimental import pallas as pl
from jax.experimental.pallas import tpu as pltpu
from jax.sharding import PartitionSpec as P

MESH = pl.DeviceIdType.MESH
F32 = jnp.float32
BF16 = jnp.bfloat16
LANES = 128
BLOCK = 256


def kernel(
    J, C, H, sub, width,
    query_ref, key_ref, value_ref, filt_ref, gain_ref, w_hbm, out_ref,
    mixed, mix_send, mix_recv, conv_send, conv_recv, gath, acc, wv, toep, filt32, xt, yt,
    w_sem, ms_sem, mr_sem, cs_sem, cr_sem, zr_sem, zs_sem, zf_sem,
):
    me = lax.axis_index("ctx")
    ch = lax.axis_index("ch")
    rows = query_ref.shape[0]
    seq = J * rows
    narrow = H * sub
    groups = narrow // width
    per = sub // width
    blocks = seq // BLOCK
    right = jnp.minimum(ch + 1, C - 1)
    left = jnp.maximum(ch - 1, 0)
    has_right = ch < C - 1
    has_left = ch > 0

    barrier = pltpu.get_barrier_semaphore()
    for o in range(1, J):
        pl.semaphore_signal(
            barrier, inc=1, device_id=(lax.rem(me + o, J), ch), device_id_type=MESH
        )

    @pl.when(has_right)
    def _():
        pl.semaphore_signal(barrier, inc=1, device_id=(me, right), device_id_type=MESH)

    @pl.when(has_left)
    def _():
        pl.semaphore_signal(barrier, inc=1, device_id=(me, left), device_id_type=MESH)

    def w_copy(s, h):
        return pltpu.make_async_copy(w_hbm.at[s, :, h], wv.at[s, h], w_sem.at[s, h])

    for h in range(H):
        for j in range(J):
            cols = slice(j * narrow + h * sub, j * narrow + (h + 1) * sub)
            part = (key_ref[:, cols].astype(F32) * value_ref[:, cols].astype(F32)).astype(BF16)
            mixed[:, cols] = part
            mix_send[h, j] = part

    pl.semaphore_wait(barrier, J - 1 + has_right.astype(jnp.int32) + has_left.astype(jnp.int32))

    def mix_copy(h, to, frm):
        return pltpu.make_async_remote_copy(
            src_ref=mix_send.at[h, to], dst_ref=mix_recv.at[h, frm],
            send_sem=ms_sem.at[h, to], recv_sem=mr_sem.at[h, frm],
            device_id=(to, ch), device_id_type=MESH,
        )

    def conv_copy(h, to, frm):
        return pltpu.make_async_remote_copy(
            src_ref=conv_send.at[h, to], dst_ref=conv_recv.at[h, frm],
            send_sem=cs_sem.at[h, to], recv_sem=cr_sem.at[h, frm],
            device_id=(to, ch), device_id_type=MESH,
        )

    for h in range(H):
        for o in range(1, J):
            mix_copy(h, lax.rem(me + o, J), me).start()
        mix_recv[h, pl.ds(me, 1)] = mix_send[h, pl.ds(me, 1)]

    for s in range(C):
        for h in range(H):
            w_copy(s, h).start()

    filt32[...] = filt_ref[me].astype(F32)
    toep[:, :, 0:LANES] = jnp.zeros((groups, LANES, LANES), BF16)

    def build(g, carry):
        row = filt32[pl.ds(g, 1), :]
        padded = jnp.concatenate([jnp.zeros((1, LANES), F32), row], axis=1)
        wide = jnp.broadcast_to(padded, (LANES, seq + LANES))
        rolled = pltpu.roll(wide, 0, 1, stride=1, stride_axis=0)
        toep[g, :, LANES:] = rolled[:, LANES:].astype(BF16)
        return carry

    lax.fori_loop(0, groups, build, 0)

    for h in range(H):
        for o in range(1, J):
            mix_copy(h, me, lax.rem(me + o, J)).wait_recv()
        flat = mix_recv[h].reshape(seq, sub)
        xt[...] = flat.T.reshape(per, width, seq)

        def group(g, carry):
            x = xt[g]
            parts = [x[:, b * BLOCK : (b + 1) * BLOCK] for b in range(blocks)]
            sums = [None] * blocks
            for d in range(blocks):
                lhs = jnp.concatenate(parts[: blocks - d], axis=0)
                at = d * BLOCK
                index = h * per + g
                rhs = jnp.concatenate(
                    [
                        toep[index, :, at + LANES : at + LANES + BLOCK],
                        toep[index, :, at : at + BLOCK],
                    ],
                    axis=0,
                )
                res = jnp.dot(lhs, rhs, preferred_element_type=F32)
                for a in range(d, blocks):
                    piece = res[(a - d) * width : (a - d + 1) * width]
                    sums[a] = piece if d == 0 else sums[a] + piece
            yt[g] = jnp.concatenate(sums, axis=1).astype(BF16)
            return carry

        lax.fori_loop(0, per, group, 0)
        back = yt[...].reshape(sub, seq).T
        conv_send[h] = back.reshape(J, rows, sub)
        for o in range(1, J):
            conv_copy(h, lax.rem(me + o, J), me).start()
        conv_recv[h, pl.ds(me, 1)] = conv_send[h, pl.ds(me, 1)]

    def z_copy(s, h, to, sems, way):
        return pltpu.make_async_remote_copy(
            src_ref=gath.at[s, h], dst_ref=gath.at[s, h],
            send_sem=sems.at[s, h], recv_sem=zr_sem.at[s, h],
            device_id=(me, to), device_id_type=MESH,
        )

    def multiply(s, h, first):
        lhs = gath[s, h]
        depth = J * sub
        cols = out_ref.shape[1]
        tile = min(512, cols)

        for n in range(cols // tile):
            at = n * tile
            rhs = wv[s, h, :, :, at : at + tile].reshape(depth, tile)
            res = jnp.dot(lhs, rhs, preferred_element_type=F32)
            if first:
                acc[:, at : at + tile] = res
            else:
                acc[:, at : at + tile] += res

    for h in range(H):
        for o in range(1, J):
            conv_copy(h, me, lax.rem(me + o, J)).wait_recv()
        pieces = []
        for j in range(J):
            cols = slice(j * narrow + h * sub, j * narrow + (h + 1) * sub)
            total = conv_recv[h, j].astype(F32) + gain_ref[:, cols] * mixed[:, cols].astype(F32)
            pieces.append((query_ref[:, cols].astype(F32) * total).astype(BF16))
        gath[pl.ds(ch, 1), h] = jnp.concatenate(pieces, axis=1)[None]

        @pl.when(has_right)
        def _():
            z_copy(ch, h, right, zs_sem, 0).start()

        @pl.when(has_left)
        def _():
            z_copy(ch, h, left, zf_sem, 1).start()

    for s in range(C):
        for h in range(H):
            w_copy(s, h).wait()
    for h in range(H):
        multiply(ch, h, h == 0)

    for step in range(1, C):
        for h in range(H):
            s_left = jnp.maximum(ch - step, 0)

            @pl.when(ch - step >= 0)
            def _():
                z_copy(s_left, h, left, zs_sem, 0).wait_recv()

                @pl.when(has_right)
                def _():
                    z_copy(s_left, h, right, zs_sem, 0).start()

            s_right = jnp.minimum(ch + step, C - 1)

            @pl.when(ch + step < C)
            def _():
                z_copy(s_right, h, right, zf_sem, 1).wait_recv()

                @pl.when(has_left)
                def _():
                    z_copy(s_right, h, left, zf_sem, 1).start()

            @pl.when(ch - step >= 0)
            def _():
                multiply(s_left, h, False)

            @pl.when(ch + step < C)
            def _():
                multiply(s_right, h, False)

    out_ref[...] = acc[...].astype(BF16)

    for h in range(H):
        for o in range(1, J):
            mix_copy(h, lax.rem(me + o, J), me).wait_send()
            conv_copy(h, lax.rem(me + o, J), me).wait_send()
        for s in range(C):

            @pl.when(has_right & (s <= ch))
            def _():
                z_copy(s, h, right, zs_sem, 0).wait_send()

            @pl.when(has_left & (s >= ch))
            def _():
                z_copy(s, h, left, zf_sem, 1).wait_send()


def shards(query_in, key_in, value_in, filters, skip_gain, out_weight):
    J = lax.axis_size("ctx")
    C = lax.axis_size("ch")
    rows, channels = query_in.shape
    seq = J * rows
    width = channels // filters.shape[0]
    narrow = channels // J
    H = 2 if (narrow // width) % 2 == 0 else 1
    sub = narrow // H
    groups = narrow // width
    per = sub // width
    outs = out_weight.shape[1]
    vmem = pl.BlockSpec(memory_space=pltpu.VMEM)
    dma = pltpu.SemaphoreType.DMA
    return pl.pallas_call(
        functools.partial(kernel, J, C, H, sub, width),
        out_shape=jax.ShapeDtypeStruct((rows, outs), BF16),
        in_specs=[vmem] * 5 + [pl.BlockSpec(memory_space=pl.ANY)],
        out_specs=vmem,
        scratch_shapes=[
            pltpu.VMEM((rows, channels), BF16),
            pltpu.VMEM((H, J, rows, sub), BF16),
            pltpu.VMEM((H, J, rows, sub), BF16),
            pltpu.VMEM((H, J, rows, sub), BF16),
            pltpu.VMEM((H, J, rows, sub), BF16),
            pltpu.VMEM((C, H, rows, J * sub), BF16),
            pltpu.VMEM((rows, outs), F32),
            pltpu.VMEM((C, H, J, sub, outs), BF16),
            pltpu.VMEM((groups, LANES, seq + LANES), BF16),
            pltpu.VMEM((groups, seq), F32),
            pltpu.VMEM((per, width, seq), BF16),
            pltpu.VMEM((per, width, seq), BF16),
            dma((C, H)),
            dma((H, J)),
            dma((H, J)),
            dma((H, J)),
            dma((H, J)),
            dma((C, H)),
            dma((C, H)),
            dma((C, H)),
        ],
        compiler_params=pltpu.CompilerParams(
            collective_id=0, has_side_effects=True, vmem_limit_bytes=60 << 20
        ),
        cost_estimate=pl.CostEstimate(
            flops=2 * rows * channels * C * outs,
            bytes_accessed=2 * channels * C * outs,
            transcendentals=0,
        ),
    )(
        query_in, key_in, value_in,
        filters.reshape(J, groups, seq),
        skip_gain.reshape(1, channels),
        out_weight.reshape(C, J, H, sub, outs),
    )


def solution(mesh):
    placed = (P("ctx", "ch"), P("ctx", "ch"), P("ctx", "ch"), P("ch", None), P("ch"), P(None, "ch"))
    return jax.shard_map(
        shards, mesh=mesh, in_specs=placed, out_specs=P("ctx", "ch"), check_vma=False
    )
```

time: 439 us -> 78.4 us (0.18)
  local copies, waits for them, and re-layouts: 279 us -> 2.09 us
  Pallas kernels: 0 us -> 76.1 us
  waiting for transfers between devices: 72.5 us -> 0 us
  matrix products: 34.2 us -> 0 us
  blocking collectives: 16.4 us -> 0 us
  between operations: 13.5 us -> 0.01 us
  starting transfers between devices: 9.44 us -> 0 us
  other arithmetic: 8.84 us -> 0 us
  loops' own time: 4.64 us -> 0 us
    reshape x6 -> x0, local copies, waits for them, and re-layouts: 144 us -> none  [the longest x3 136 us: toeplitz(): repeated[:, out_rows - 1:out_rows - 1 + out_rows * width]]
    while x10 -> x0, local copies, waits for them, and re-layouts: 92.3 us -> none
    pallas_call x0 -> x1, Pallas kernels: none -> 76.1 us  [shards(): pl.pallas_call(functools.partial(kernel, J, C, H, sub, width), out_shape=...]
    all_gather x1 -> x0, waiting for transfers between devices: 63 us -> none  [project(): lax.all_gather(gated, 'ch', axis=1, tiled=True)]
    slice x3 -> x0, local copies, waits for them, and re-layouts: 25.3 us -> none  [toeplitz(): repeated[:, out_rows - 1:out_rows - 1 + out_rows * width]]
    while x3 -> x0, matrix products: 18.5 us -> none
    all_to_all x1 -> x0, blocking collectives: 16.4 us -> none  [shards(): lax.all_to_all(gated_ch, 'ctx', split_axis=0, concat_axis=1, tiled=True)]
    dot_general x1 -> x0, matrix products: 15.7 us -> none  [project(): jnp.dot(lax.all_gather(gated, 'ch', axis=1, tiled=True), out_weight, pref...]
  transfers between devices with their start and end apart: 3 -> 0, of which waited for: 2 -> 0; matrix products, arithmetic and copies ran while one was open for 68% -> 0% of each run, Pallas kernels for 0% -> 0%
where the time goes in v1:
time: 78.4 us; the launch traced here: 78.2 us
  Pallas kernels  76.1 us (97%)
  local copies, waits for them, and re-layouts  2.09 us (3%)
    pallas_call x1, Pallas kernels, shards(): pl.pallas_call(functools.partial(kernel, J, C, H, sub, width), out_shape=...  76.1 us
    unnamed x1, local copies, waits for them, and re-layouts  2.09 us

profile of v1, /device:TPU:0, one launch (start us, length us, event | category | flops | bytes accessed | tf_op | source)
XLA Modules:
  0.0 78.2 jit_solution(4629067258420965873)
XLA Ops:
  0.0 76.1 %shard_map.64 = bf16[192,2048]{1,0:T(8,128)(2,1)} custom-call(bf16[192,2048]{1,0:T(8,128)(2,1)} %query_ref.1, bf16[192,2048]{1,0:T(8,128)(2,1)} %key_ref.1, bf16[192,2048]{1,0:T(8,128)(2,1)} %value_ref.1, bf16[8,16,1536]{2,1,0:T(8,128)(2,1)} %bitcast.4, f32[1,2048]{1,0:T(1,128)} %bitcast.5, bf16[4,8,2,128,2048]{4,3,2,1,0:T(8,128)(2,1)} %bitcast.3), custom_call_target="tpu_custom_call" | custom-call | flops 6442450944 | bytes 33554432 | tf_op jit(solution)/shard_map/pallas_call | solution.py:240
  76.1 2.1 %copy.8 = bf16[192,2048]{1,0:T(8,128)(2,1)} copy(bf16[192,2048]{1,0:T(8,128)(2,1)} %shard_map.64) | data formatting | bytes 1572864

commit v2 on v1

--- a/solution.py
+++ b/solution.py
@@ -17,7 +17,7 @@
 def kernel(
     J, C, H, sub, width,
     query_ref, key_ref, value_ref, filt_ref, gain_ref, w_hbm, out_ref,
-    mixed, mix_send, mix_recv, conv_send, conv_recv, gath, acc, wv, toep, filt32, xt, yt,
+    gcol, mix_send, mix_recv, conv_send, conv_recv, gath, acc, wv, toep, filt32, xt, yt,
     w_sem, ms_sem, mr_sem, cs_sem, cr_sem, zr_sem, zs_sem, zf_sem,
 ):
     me = lax.axis_index("ctx")
@@ -50,14 +50,25 @@
     def w_copy(s, h):
         return pltpu.make_async_copy(w_hbm.at[s, :, h], wv.at[s, h], w_sem.at[s, h])
 
-    for h in range(H):
+    pack = mix_send.shape[3] // sub
+    short = rows // pack
+
+    def fold(part):
+        cuts = [part[..., i * short : (i + 1) * short, :] for i in range(pack)]
+        return jnp.concatenate(cuts, axis=-1) if pack > 1 else part
+
+    def unfold(part):
+        cuts = [part[..., i * sub : (i + 1) * sub] for i in range(pack)]
+        return jnp.concatenate(cuts, axis=-2) if pack > 1 else part
+
+    def columns(h, j):
+        return slice(j * narrow + h * sub, j * narrow + (h + 1) * sub)
+
+    def mix(h):
         for j in range(J):
-            cols = slice(j * narrow + h * sub, j * narrow + (h + 1) * sub)
+            cols = columns(h, j)
             part = (key_ref[:, cols].astype(F32) * value_ref[:, cols].astype(F32)).astype(BF16)
-            mixed[:, cols] = part
-            mix_send[h, j] = part
-
-    pl.semaphore_wait(barrier, J - 1 + has_right.astype(jnp.int32) + has_left.astype(jnp.int32))
+            mix_send[h, j] = fold(part)
 
     def mix_copy(h, to, frm):
         return pltpu.make_async_remote_copy(
@@ -73,10 +84,19 @@
             device_id=(to, ch), device_id_type=MESH,
         )
 
-    for h in range(H):
+    def send_mix(h):
         for o in range(1, J):
             mix_copy(h, lax.rem(me + o, J), me).start()
         mix_recv[h, pl.ds(me, 1)] = mix_send[h, pl.ds(me, 1)]
+
+    mix(0)
+    pl.semaphore_wait(barrier, J - 1 + has_right.astype(jnp.int32) + has_left.astype(jnp.int32))
+
+    send_mix(0)
+    for h in range(1, H):
+        mix(h)
+        if h == 1:
+            send_mix(1)
 
     for s in range(C):
         for h in range(H):
@@ -84,31 +104,27 @@
 
     filt32[...] = filt_ref[me].astype(F32)
     toep[:, :, 0:LANES] = jnp.zeros((groups, LANES, LANES), BF16)
-
-    def build(g, carry):
-        row = filt32[pl.ds(g, 1), :]
-        padded = jnp.concatenate([jnp.zeros((1, LANES), F32), row], axis=1)
-        wide = jnp.broadcast_to(padded, (LANES, seq + LANES))
-        rolled = pltpu.roll(wide, 0, 1, stride=1, stride_axis=0)
-        toep[g, :, LANES:] = rolled[:, LANES:].astype(BF16)
-        return carry
-
-    lax.fori_loop(0, groups, build, 0)
-
-    for h in range(H):
-        for o in range(1, J):
-            mix_copy(h, me, lax.rem(me + o, J)).wait_recv()
-        flat = mix_recv[h].reshape(seq, sub)
+    gain = jnp.broadcast_to(gain_ref[me], (LANES, narrow))
+    gcol[...] = gain.T.reshape(groups, width, LANES)
+
+    def build(h):
+        for g in range(h * per, (h + 1) * per):
+            padded = jnp.concatenate([jnp.zeros((1, LANES), F32), filt32[g : g + 1, :]], axis=1)
+            wide = jnp.broadcast_to(padded, (LANES, seq + LANES))
+            rolled = pltpu.roll(wide, 0, 1, stride=1, stride_axis=0)
+            toep[g, :, LANES:] = rolled[:, LANES:].astype(BF16)
+
+    def convolve(h):
+        flat = unfold(mix_recv[h]).reshape(seq, sub)
         xt[...] = flat.T.reshape(per, width, seq)
-
-        def group(g, carry):
+        for g in range(per):
+            index = h * per + g
             x = xt[g]
             parts = [x[:, b * BLOCK : (b + 1) * BLOCK] for b in range(blocks)]
             sums = [None] * blocks
             for d in range(blocks):
                 lhs = jnp.concatenate(parts[: blocks - d], axis=0)
                 at = d * BLOCK
-                index = h * per + g
                 rhs = jnp.concatenate(
                     [
                         toep[index, :, at + LANES : at + LANES + BLOCK],
@@ -120,12 +136,10 @@
                 for a in range(d, blocks):
                     piece = res[(a - d) * width : (a - d + 1) * width]
                     sums[a] = piece if d == 0 else sums[a] + piece
-            yt[g] = jnp.concatenate(sums, axis=1).astype(BF16)
-            return carry
-
-        lax.fori_loop(0, per, group, 0)
+            gain = gcol[index][:, 0:1]
+            yt[g] = (jnp.concatenate(sums, axis=1) + gain * x.astype(F32)).astype(BF16)
         back = yt[...].reshape(sub, seq).T
-        conv_send[h] = back.reshape(J, rows, sub)
+        conv_send[h] = fold(back.reshape(J, rows, sub))
         for o in range(1, J):
             conv_copy(h, lax.rem(me + o, J), me).start()
         conv_recv[h, pl.ds(me, 1)] = conv_send[h, pl.ds(me, 1)]
@@ -152,14 +166,13 @@
             else:
                 acc[:, at : at + tile] += res
 
-    for h in range(H):
+    def gate(h):
         for o in range(1, J):
             conv_copy(h, me, lax.rem(me + o, J)).wait_recv()
         pieces = []
         for j in range(J):
-            cols = slice(j * narrow + h * sub, j * narrow + (h + 1) * sub)
-            total = conv_recv[h, j].astype(F32) + gain_ref[:, cols] * mixed[:, cols].astype(F32)
-            pieces.append((query_ref[:, cols].astype(F32) * total).astype(BF16))
+            total = unfold(conv_recv[h, j]).astype(F32)
+            pieces.append((query_ref[:, columns(h, j)].astype(F32) * total).astype(BF16))
         gath[pl.ds(ch, 1), h] = jnp.concatenate(pieces, axis=1)[None]
 
         @pl.when(has_right)
@@ -169,6 +182,19 @@
         @pl.when(has_left)
         def _():
             z_copy(ch, h, left, zf_sem, 1).start()
+
+    build(0)
+    for h in range(H):
+        for o in range(1, J):
+            mix_copy(h, me, lax.rem(me + o, J)).wait_recv()
+        convolve(h)
+        if h + 1 < H:
+            if h + 2 < H:
+                send_mix(h + 2)
+            build(h + 1)
+        if h > 0:
+            gate(h - 1)
+    gate(H - 1)
 
     for s in range(C):
         for h in range(H):
@@ -230,8 +256,16 @@
     seq = J * rows
     width = channels // filters.shape[0]
     narrow = channels // J
-    H = 2 if (narrow // width) % 2 == 0 else 1
+    H = 1
+    for cut in (2, 4):
+        part = narrow // cut
+        fits = LANES % part == 0 and rows % (16 * (LANES // part)) == 0
+        if (narrow // width) % cut == 0 and (part % LANES == 0 or fits):
+            H = cut
     sub = narrow // H
+    pack = max(1, LANES // sub)
+    if rows % (16 * pack):
+        pack = 1
     groups = narrow // width
     per = sub // width
     outs = out_weight.shape[1]
@@ -243,11 +277,11 @@
         in_specs=[vmem] * 5 + [pl.BlockSpec(memory_space=pl.ANY)],
         out_specs=vmem,
         scratch_shapes=[
-            pltpu.VMEM((rows, channels), BF16),
-            pltpu.VMEM((H, J, rows, sub), BF16),
-            pltpu.VMEM((H, J, rows, sub), BF16),
-            pltpu.VMEM((H, J, rows, sub), BF16),
-            pltpu.VMEM((H, J, rows, sub), BF16),
+            pltpu.VMEM((groups, width, LANES), F32),
+            pltpu.VMEM((H, J, rows // pack, sub * pack), BF16),
+            pltpu.VMEM((H, J, rows // pack, sub * pack), BF16),
+            pltpu.VMEM((H, J, rows // pack, sub * pack), BF16),
+            pltpu.VMEM((H, J, rows // pack, sub * pack), BF16),
             pltpu.VMEM((C, H, rows, J * sub), BF16),
             pltpu.VMEM((rows, outs), F32),
             pltpu.VMEM((C, H, J, sub, outs), BF16),
@@ -275,7 +309,7 @@
     )(
         query_in, key_in, value_in,
         filters.reshape(J, groups, seq),
-        skip_gain.reshape(1, channels),
+        skip_gain.reshape(J, 1, narrow),
         out_weight.reshape(C, J, H, sub, outs),
     )
 

time: 78.4 us -> 74.8 us (0.954)
  Pallas kernels: 76.1 us -> 72.5 us
    pallas_call x1, Pallas kernels: 76.1 us -> 72.5 us  [shards(): pl.pallas_call(functools.partial(kernel, J, C, H, sub, width), out_shape=...]
where the time goes in v2:
time: 74.8 us; the launch traced here: 74.6 us
  Pallas kernels  72.5 us (97%)
  local copies, waits for them, and re-layouts  2.09 us (3%)
    pallas_call x1, Pallas kernels, shards(): pl.pallas_call(functools.partial(kernel, J, C, H, sub, width), out_shape=...  72.5 us
    unnamed x1, local copies, waits for them, and re-layouts  2.09 us

profile of v2, /device:TPU:0, one launch (start us, length us, event | category | flops | bytes accessed | tf_op | source)
XLA Modules:
  0.0 74.6 jit_solution(1741895788140993071)
XLA Ops:
  0.0 72.5 %shard_map.64 = bf16[192,2048]{1,0:T(8,128)(2,1)} custom-call(bf16[192,2048]{1,0:T(8,128)(2,1)} %query_ref.1, bf16[192,2048]{1,0:T(8,128)(2,1)} %key_ref.1, bf16[192,2048]{1,0:T(8,128)(2,1)} %value_ref.1, bf16[8,16,1536]{2,1,0:T(8,128)(2,1)} %bitcast.4, f32[8,1,256]{2,1,0:T(1,128)} %bitcast.5, bf16[4,8,4,64,2048]{4,3,2,1,0:T(8,128)(2,1)} %bitcast.3), custom_call_target="tpu_custom_call" | custom-call | flops 6442450944 | bytes 33554432 | tf_op jit(solution)/shard_map/pallas_call | solution.py:274
  72.5 2.1 %copy.8 = bf16[192,2048]{1,0:T(8,128)(2,1)} copy(bf16[192,2048]{1,0:T(8,128)(2,1)} %shard_map.64) | data formatting | bytes 1572864

commit v3 on v2

--- a/solution.py
+++ b/solution.py
@@ -183,6 +183,26 @@
         def _():
             z_copy(ch, h, left, zf_sem, 1).start()
 
+    def forward(step, h):
+        s_left = jnp.maximum(ch - step, 0)
+        s_right = jnp.minimum(ch + step, C - 1)
+
+        @pl.when(ch - step >= 0)
+        def _():
+            z_copy(s_left, h, left, zs_sem, 0).wait_recv()
+
+            @pl.when(has_right)
+            def _():
+                z_copy(s_left, h, right, zs_sem, 0).start()
+
+        @pl.when(ch + step < C)
+        def _():
+            z_copy(s_right, h, right, zf_sem, 1).wait_recv()
+
+            @pl.when(has_left)
+            def _():
+                z_copy(s_right, h, left, zf_sem, 1).start()
+
     build(0)
     for h in range(H):
         for o in range(1, J):
@@ -194,6 +214,8 @@
             build(h + 1)
         if h > 0:
             gate(h - 1)
+        if h > 2 and C > 1:
+            forward(1, h - 3)
     gate(H - 1)
 
     for s in range(C):
@@ -205,24 +227,9 @@
     for step in range(1, C):
         for h in range(H):
             s_left = jnp.maximum(ch - step, 0)
-
-            @pl.when(ch - step >= 0)
-            def _():
-                z_copy(s_left, h, left, zs_sem, 0).wait_recv()
-
-                @pl.when(has_right)
-                def _():
-                    z_copy(s_left, h, right, zs_sem, 0).start()
-
             s_right = jnp.minimum(ch + step, C - 1)
-
-            @pl.when(ch + step < C)
-            def _():
-                z_copy(s_right, h, right, zf_sem, 1).wait_recv()
-
-                @pl.when(has_left)
-                def _():
-                    z_copy(s_right, h, left, zf_sem, 1).start()
+            if step > 1 or h >= max(0, H - 3):
+                forward(step, h)
 
             @pl.when(ch - step >= 0)
             def _():
@@ -257,7 +264,7 @@
     width = channels // filters.shape[0]
     narrow = channels // J
     H = 1
-    for cut in (2, 4):
+    for cut in (2, 4, 8):
         part = narrow // cut
         fits = LANES % part == 0 and rows % (16 * (LANES // part)) == 0
         if (narrow // width) % cut == 0 and (part % LANES == 0 or fits):

time: 74.8 us -> 75.7 us (1.012)
  Pallas kernels: 72.5 us -> 73.4 us
    pallas_call x1, Pallas kernels: 72.5 us -> 73.4 us  [shards(): pl.pallas_call(functools.partial(kernel, J, C, H, sub, width), out_shape=...]
where the time goes in v3:
time: 75.7 us; the launch traced here: 75.5 us
  Pallas kernels  73.4 us (97%)
  local copies, waits for them, and re-layouts  2.09 us (3%)
    pallas_call x1, Pallas kernels, shards(): pl.pallas_call(functools.partial(kernel, J, C, H, sub, width), out_shape=...  73.4 us
    unnamed x1, local copies, waits for them, and re-layouts  2.09 us

profile of v3, /device:TPU:0, one launch (start us, length us, event | category | flops | bytes accessed | tf_op | source)
XLA Modules:
  0.0 75.5 jit_solution(5327824149994135)
XLA Ops:
  0.0 73.4 %shard_map.64 = bf16[192,2048]{1,0:T(8,128)(2,1)} custom-call(bf16[192,2048]{1,0:T(8,128)(2,1)} %query_ref.1, bf16[192,2048]{1,0:T(8,128)(2,1)} %key_ref.1, bf16[192,2048]{1,0:T(8,128)(2,1)} %value_ref.1, bf16[8,16,1536]{2,1,0:T(8,128)(2,1)} %bitcast.4, f32[8,1,256]{2,1,0:T(1,128)} %bitcast.5, bf16[4,8,8,32,2048]{4,3,2,1,0:T(8,128)(2,1)} %bitcast.3), custom_call_target="tpu_custom_call" | custom-call | flops 6442450944 | bytes 33554432 | tf_op jit(solution)/shard_map/pallas_call | solution.py:281
  73.4 2.1 %copy.8 = bf16[192,2048]{1,0:T(8,128)(2,1)} copy(bf16[192,2048]{1,0:T(8,128)(2,1)} %shard_map.64) | data formatting | bytes 1572864
